TPU v7x, 256 devices: a whole 4x4x8 slice. The times are simulated.
256 devices in a mesh: shard: 64 (over z, x, core), rep: 4 (over y).
Axes of the slice: x: 4, y: 4, z: 8, core: 2. Of those that a mesh axis runs over, the one named last changes fastest.
Arguments:
- embeddings: bfloat16 [409600, 1024], P('shard'), may hold values from -6 to 6
- send_index: int32 [409600], P('shard'), may hold values from 0 to 6399, as said below
- place_index: int32 [409600], P('shard'), may hold values from 0 to 6654, as said below
- slot_cluster: int32 [425984], P('shard'), may hold values from -1 to 1663, as said below
- pair_list: int32 [22528, 2], P(('shard', 'rep')), may hold values from 0 to 25, as said below
Outputs:
- best_cosine: float32 [409600], P('shard')
Inputs may be any that keep to these rules, and one draw needn't show every extreme that they name: `send_index`: on each device, the entries o * 100 to (o + 1) * 100 - 1 of its block are the local documents sent to owner o; the device's 64 * 100 entries are a permutation of its 6400 documents, so each device sends exactly 100 documents to each owner. `place_index`: on each owner, the 6400 entries are distinct slots, exactly the slots whose slot_cluster is not -1. `slot_cluster`: an owner's 26 * 256 slots form 26 blocks of 256; it holds two or more clusters, each filling one or more consecutive whole blocks with its members first and 1 to 255 padding slots (-1) at the end of its last block, 256 padding slots in all. Ids of owner o lie in o * 26 to o * 26 + 25. `pair_list`: row (o * 4 + r) * 88 + p holds a pair (i, j), i <= j, of blocks of owner o that belong to one cluster; over its 352 rows, owner o lists every such pair at least once, some of them more than once.
All inputs are finite; a program needn't handle non-finite values.
Results may differ from a plain program's by a relative error of at most 0.0014.
Values may be sent and summed in bfloat16 or wider, within the bound.
A program may use at most 128 MiB of HBM per device.

v0:
```python
import jax
import jax.numpy as jnp
from jax import lax
from jax.sharding import PartitionSpec as P

D = 1024
BLK = 256


def shards(embeddings, send_index, place_index, slot_cluster, pair_list):
    owners = lax.axis_size("shard")
    share = send_index.shape[0] // owners
    blocks_held = slot_cluster.shape[0] // BLK
    wide = embeddings.astype(jnp.float32)
    normed = (wide * lax.rsqrt(jnp.sum(wide * wide, axis=1, keepdims=True) + 1e-06)).astype(
        jnp.bfloat16
    )
    outgoing = normed[send_index].reshape(owners, share, D)
    arrived = lax.all_to_all(outgoing, "shard", split_axis=0, concat_axis=0, tiled=True)
    slots = (
        jnp.zeros((blocks_held * BLK, D), jnp.bfloat16).at[place_index].set(arrived.reshape(-1, D))
    )
    blocks = slots.reshape(blocks_held, BLK, D)
    cluster_blocks = slot_cluster.reshape(blocks_held, BLK)
    groups = pair_list.reshape(-1, 8, 2)
    diagonal = jnp.eye(BLK, dtype=bool)

    def visit(best, group):
        first = group[:, 0]
        second = group[:, 1]
        gram = jnp.einsum(
            "pad,pbd->pab", blocks[first], blocks[second], preferred_element_type=jnp.float32
        )
        left = cluster_blocks[first]
        right = cluster_blocks[second]
        counts = (left[:, :, None] == right[:, None, :]) & (left[:, :, None] >= 0)
        counts = counts & ~((first == second)[:, None, None] & diagonal[None, :, :])
        values = jnp.where(counts, gram, jnp.float32(-1.0))
        best = best.at[first].max(jnp.max(values, axis=2))
        best = best.at[second].max(jnp.max(values, axis=1))
        return (best, None)

    start = jnp.full((blocks_held, BLK), -1.0, jnp.float32)
    best_flat = lax.scan(visit, start, groups)[0].reshape(-1)
    merged = lax.pmax(best_flat, "rep")
    outbound = merged[place_index].reshape(owners, share)
    returned = lax.all_to_all(outbound, "shard", split_axis=0, concat_axis=0, tiled=True)
    result = jnp.zeros((embeddings.shape[0],), jnp.float32).at[send_index].set(returned.reshape(-1))
    return result


def solution(mesh):
    return jax.shard_map(
        shards,
        mesh=mesh,
        in_specs=(P("shard", None), P("shard"), P("shard"), P("shard"), P(("shard", "rep"), None)),
        out_specs=P("shard"),
        check_vma=False,
    )
```

profile of v0, /device:TPU:1, one launch (start us, length us, event | category | flops | bytes accessed | tf_op | source)
XLA Modules:
  0.0 802.1 jit_solution(5647493465010741807)
XLA Ops:
  8.1 11.7 %fusion.5 = bf16[6400,1024]{1,0:T(8,128)(2,1)} fusion(bf16[6400,1024]{1,0:T(8,128)(2,1)} %param.7, f32[6400]{0:T(1024)S(1)} %add_rsqrt_fusion), kind=kLoop, calls=%fused_computation.25 | loop fusion | flops 19660800 | bytes 26240000 | tf_op jit(solution)/shard_map/convert_element_type | solution.py:15
  19.9 34.7 %gather_fusion.4 = bf16[6400,1024]{1,0:T(8,128)(2,1)} fusion(bf16[6400,1024]{1,0:T(8,128)(2,1)} %fusion.5, s32[7168]{0:T(1024)S(1)} %pad_clamp_fusion.3), kind=kCustom, calls=%fused_computation.4 | custom fusion | bytes 26240000 | tf_op jit(solution)/shard_map/gather | solution.py:18
  54.5 16.1 %reshape.51 = bf16[64,100,1024]{2,1,0:T(8,128)(2,1)} reshape(bf16[6400,1024]{1,0:T(8,128)(2,1)} %gather_fusion.4) | data formatting | bytes 26214400 | tf_op jit(solution)/shard_map/reshape | solution.py:18
  70.6 13.3 %all-to-all-start = ((bf16[64,100,1024]{2,1,0:T(8,128)(2,1)}), bf16[64,100,1024]{2,1,0:T(8,128)(2,1)}, u32[]{:S(2)}, u32[]{:S(2)}) async-start(bf16[64,100,1024]{2,1,0:T(8,128)(2,1)} %reshape.51), calls=%async_computation | async-start | bytes 27262976 | tf_op jit(solution)/shard_map/all_to_all | solution.py:19
  84.1 297.3 %all-to-all-done = bf16[64,100,1024]{2,1,0:T(8,128)(2,1)} async-done(((bf16[64,100,1024]{2,1,0:T(8,128)(2,1)}), bf16[64,100,1024]{2,1,0:T(8,128)(2,1)}, u32[]{:S(2)}, u32[]{:S(2)}) %all-to-all-start) | async-done | bytes 13107232 | tf_op jit(solution)/shard_map/all_to_all | solution.py:19
  381.4 16.2 %reshape.124 = bf16[6400,1024]{1,0:T(8,128)(2,1)} reshape(bf16[64,100,1024]{2,1,0:T(8,128)(2,1)} %all-to-all-done) | data formatting | bytes 26214400 | tf_op jit(solution)/shard_map/reshape | solution.py:21
  397.5 41.2 %scatter_custom_fusion.2 = bf16[6656,1024]{1,0:T(8,128)(2,1)} fusion(s32[6400]{0:T(1024)S(1)} %compare_select_fusion.2, bf16[6400,1024]{1,0:T(8,128)(2,1)} %reshape.124, bf16[]{:T(256)} %constant.23.clone.1), kind=kCustom, calls=%fused_computation.26 | custom fusion | bytes 13632000 | tf_op jit(solution)/shard_map/scatter | solution.py:21
  438.8 266.5 %while.11 = (s32[]{:T(128)}, f32[26,256]{1,0:T(8,128)S(1)}, s32[11,8,2]{1,0,2:T(8,128)S(1)}, s32[26,256]{1,0:T(8,128)S(1)}, bf16[26,256,1024]{2,1,0:T(8,128)(2,1)}, /*index=5*/s32[]{:T(128)}) while((s32[]{:T(128)}, f32[26,256]{1,0:T(8,128)S(1)}, s32[11,8,2]{1,0,2:T(8,128)S(1)}, s32[26,256]{1,0:T(8,128)S(1)}, ...), condition=%wide.region_7.8_spmd.clone, body=%wide.region_2.7_spmd.clone.sunk | while | flops 1078005760 | bytes 25432728 | solution.py:44
  439.4 7.6 gather_fusion
  447.0 7.7 gather_fusion.1
  463.6 7.6 gather_fusion
  471.2 7.7 gather_fusion.1
  487.8 7.6 gather_fusion
  495.5 7.7 gather_fusion.1
  512.1 7.6 gather_fusion
  519.7 7.7 gather_fusion.1
  536.3 7.6 gather_fusion
  543.9 7.7 gather_fusion.1
  560.5 7.6 gather_fusion
  568.1 7.7 gather_fusion.1
  584.7 7.6 gather_fusion
  592.4 7.7 gather_fusion.1
  609.0 7.6 gather_fusion
  616.6 7.7 gather_fusion.1
  633.2 7.6 gather_fusion
  640.8 7.7 gather_fusion.1
  665.1 7.7 gather_fusion.1
  689.3 7.7 gather_fusion.1
  705.3 13.6 %pmax.7 = f32[6656]{0:T(1024)S(1)} all-reduce(f32[6656]{0:T(1024)S(1)} %reshape.54), channel_id=1, replica_groups=mesh['shard'=64,'rep'=4] {'rep'}, use_global_device_ids=true, to_apply=%region_8.9 | all-reduce | flops 6656 | bytes 53248 | tf_op jit(solution)/shard_map/pmax | solution.py:45
  718.8 33.2 %gather_fusion.5 = f32[6400]{0:T(1024)S(1)} fusion(f32[6656]{0:T(1024)S(1)} %pmax.7, s32[7168]{0:T(1024)S(1)} %pad_clamp_fusion.2), kind=kCustom, calls=%fused_computation.5 | custom fusion | bytes 76800 | tf_op jit(solution)/shard_map/gather | solution.py:46
  752.2 24.0 %all_to_all.14 = f32[64,1,100]{2,1,0:T(1,128)S(1)} all-to-all(f32[64,1,100]{2,1,0:T(1,128)S(1)} %all_to_all.10), channel_id=1, replica_groups=mesh['shard'=64,'rep'=4] {'shard'}, dimensions={0} | all-to-all | bytes 51200 | tf_op jit(solution)/shard_map/all_to_all | solution.py:47
  777.6 24.5 %scatter_custom_fusion.3 = f32[6400]{0:T(1024)} fusion(s32[6400]{0:T(1024)S(1)} %compare_select_fusion.3, f32[6400]{0:T(1024)S(1)} %reshape.132, f32[]{:T(128)} %constant.3.clone.1), kind=kCustom, calls=%fused_computation.33 | custom fusion | bytes 25604 | tf_op jit(solution)/shard_map/scatter | solution.py:48
  (143 shorter events, 122.0 us)
Async XLA Ops:
  70.6 13.3 %copy-start.1 = (s32[6656]{0:T(1024)S(1)}, s32[6656]{0:T(1024)}, u32[]{:S(2)}) copy-start(s32[6656]{0:T(1024)} %param.10) | copy-start | bytes 79876
  70.6 13.3 %copy-start.2 = (s32[88,2]{0,1:T(2,128)S(1)}, s32[88,2]{0,1:T(2,128)}, u32[]{:S(2)}) copy-start(s32[88,2]{0,1:T(2,128)} %param.11) | copy-start | bytes 2116
  70.6 13.4 %copy-start = (s32[6400]{0:T(1024)S(1)}, s32[6400]{0:T(1024)}, u32[]{:S(2)}) copy-start(s32[6400]{0:T(1024)} %param.9) | copy-start | bytes 76804
  70.6 310.8 %all-to-all-start = ((bf16[64,100,1024]{2,1,0:T(8,128)(2,1)}), bf16[64,100,1024]{2,1,0:T(8,128)(2,1)}, u32[]{:S(2)}, u32[]{:S(2)}) async-start(bf16[64,100,1024]{2,1,0:T(8,128)(2,1)} %reshape.51), calls=%async_computation | async-start | bytes 27262976 | tf_op jit(solution)/shard_map/all_to_all | solution.py:19
where the time goes:
time: 804 us; the launch traced here: 802 us
  local copies, waits for them, and re-layouts  348 us (43%)
  waiting for transfers between devices  297 us (37%)
  matrix products  68.8 us (9%)
  blocking collectives  37.6 us (5%)
  other arithmetic  36.4 us (5%)
  starting transfers between devices  13.3 us (2%)
    all_to_all x1, waiting for transfers between devices, shards(): lax.all_to_all(outgoing, 'shard', split_axis=0, concat_axis=0, tiled=True)  297 us
    gather x11, local copies, waits for them, and re-layouts, visit(): blocks[second]  84.6 us
    gather x11, local copies, waits for them, and re-layouts, visit(): blocks[first]  83.9 us
    dot_general x11, matrix products, visit(): jnp.einsum('pad,pbd->pab', blocks[first], blocks[second], preferred_eleme...  68.8 us
    scatter x1, local copies, waits for them, and re-layouts, shards(): jnp.zeros((blocks_held * BLK, D), jnp.bfloat16).at[place_index]  41.2 us
    gather x1, local copies, waits for them, and re-layouts, shards(): outgoing = normed[send_index].reshape(owners, share, D)  34.7 us
    gather x1, local copies, waits for them, and re-layouts, shards(): outbound = merged[place_index].reshape(owners, share)  33.2 us
    scatter x1, local copies, waits for them, and re-layouts, shards(): jnp.zeros((embeddings.shape[0],), jnp.float32).at[send_index]  24.5 us
  transfers between devices with their start and end apart: 1, of which 1 were waited for; matrix products, arithmetic and copies ran while one was open for 0% of the time, Pallas kernels for 0%

commit v1 on v0

v1 whole, which is shorter than its diff:
```python
import functools

import jax
import jax.numpy as jnp
from jax import lax
from jax.experimental import pallas as pl
from jax.experimental.pallas import tpu as pltpu
from jax.sharding import PartitionSpec as P

D = 1024
BLK = 256
DOCS = 6400
NS = 64
NR = 4
SHARE = 100
PART = 25
PADDED = 26
MSG = PADDED * 8
GROUP = PADDED * 8
NG = 8
CHUNK = 400
NCHUNK = DOCS // CHUNK
STG = 0
CS = 2048
RA = 8192
MESH = pl.DeviceIdType.MESH
F32 = jnp.float32
BF16 = jnp.bfloat16
LAST = (((1,), (1,)), ((), ()))


def pieces(v):
    a = v.astype(BF16).astype(F32)
    r = v - a
    b = r.astype(BF16).astype(F32)
    return a, b, r - b


def kernel(
    send_ref, table_ref, emb_ref, idx_ref, place_ref, out_ref,
    wide, q, outb, recv, emb, colacc, cl, ctmp, lhs, rhs, tsrc, trecv, trow, vrecv,
    esem, zsend, zrecv, ysend, yrecv, r1send, r1recv, r2send, r2recv,
):
    me = lax.axis_index("shard")
    rep = lax.axis_index("rep")
    z, x, c = me // 8, (me // 2) % 4, me % 2
    role = jnp.where(c == 0, rep, 3 - rep)
    odd = role % 2

    def rep_of(r):
        r = (r + 4) % 4
        return jnp.where(c == 0, r, 3 - r)

    own_pos = jnp.where(role == 3, 1, 0)
    first_pos = jnp.where(role == 0, 0, 1)
    second_to = jnp.where(role == 2, rep_of(3), rep_of(1))
    y0 = jnp.where(role == 3, rep_of(0), rep_of(role))
    y1 = jnp.where(role == 3, rep_of(3), rep_of(role + 1))
    y2 = jnp.where(role == 1, rep_of(3), jnp.where(role == 3, rep_of(2), -1))

    def fetch(ch, slot):
        return pltpu.make_async_copy(
            emb_ref.at[pl.ds(pl.multiple_of(ch * CHUNK, 16), CHUNK)], emb.at[slot], esem.at[slot]
        )

    fetch(0, 0).start()
    fetch(1, 1).start()

    barrier = pltpu.get_barrier_semaphore()

    @pl.loop(1, NS)
    def _(k):
        pl.semaphore_signal(barrier, inc=1, device_id={"shard": (me + k) % NS}, device_id_type=MESH)

    for k in range(1, NR):
        pl.semaphore_signal(barrier, inc=1, device_id={"rep": (rep + k) % NR}, device_id_type=MESH)

    @pl.loop(0, NCHUNK)
    def _(ch):
        slot = ch % 2
        fetch(ch, slot).wait()

        @pl.loop(0, CHUNK // 16, unroll=5)
        def _(r):
            rows = emb[slot, pl.ds(pl.multiple_of(r * 16, 16), 16), :].astype(F32)
            base = ch * (CHUNK * 8) + r * 128
            for h in range(2):
                for j in range(8):
                    wide[pl.ds(pl.multiple_of(base + h * 64 + j * 8, 8), 8), :] = rows[
                        8 * h : 8 * h + 8, 128 * j : 128 * j + 128
                    ]

        @pl.when(ch + 2 < NCHUNK)
        def _():
            fetch(ch + 2, slot).start()

    pl.semaphore_wait(barrier, NS - 1 + NR - 1)

    def zcopy(dst):
        return pltpu.make_async_remote_copy(
            src_ref=outb.at[dst], dst_ref=recv.at[me], send_sem=zsend.at[dst], recv_sem=zrecv.at[me],
            device_id={"shard": dst}, device_id_type=MESH,
        )

    def zlocal():
        return pltpu.make_async_copy(outb.at[me], recv.at[me], zrecv.at[me])

    def address(i):
        return (i // 8) * 64 + i % 8

    @pl.loop(0, NS)
    def _(k):
        t, h, w, b = k // 16, (k // 8) % 2, (k // 2) % 4, k % 2
        dst = ((z + h + 2 * w) % 8) * 8 + ((x + t) % 4) * 2 + (c + b) % 2
        base = dst * SHARE + rep * PART
        for a in range(PADDED // 2):
            i0 = send_ref[base + 2 * a]
            i1 = send_ref[base + min(2 * a + 1, PART - 1)]
            v0 = wide[pl.ds(address(i0), 8, stride=8), :]
            v1 = wide[pl.ds(address(i1), 8, stride=8), :]
            outb[dst, pl.ds(16 * a, 16), :] = jnp.concatenate([v0, v1], axis=0).astype(BF16)

        @pl.when(dst != me)
        def _():
            zcopy(dst).start()

        @pl.when(dst == me)
        def _():
            zlocal().start()

    place = place_ref[...]
    block = place // BLK
    ids = jnp.full((NS, 128), -1.0, F32)
    for b in range(table_ref.shape[0] // BLK):
        ids = jnp.where(block == b, (table_ref[b * BLK] - me * 26).astype(F32), ids)
    ids = jnp.where(place >= 0, ids, -1.0)
    ctmp[...] = ids
    for g in range(NG):
        for e in range(8):
            s = ((e // 2) * 2 + g % 2) * 8 + (g // 2) * 2 + e % 2
            tsrc[8 * g + e : 8 * g + e + 1, :] = ctmp[s : s + 1, :]
    ordered = tsrc[...].astype(BF16)
    lane = lax.broadcasted_iota(jnp.int32, (128, 256), 0)
    spot = lax.broadcasted_iota(jnp.int32, (128, 256), 1)
    keep = (lax.broadcasted_iota(jnp.int32, (NS, 256), 1) % 8) == (
        lax.broadcasted_iota(jnp.int32, (NS, 256), 0) % 8
    )
    for y in range(NR):
        spread = (lane == 32 * y + spot // 8).astype(F32).astype(BF16)
        ids_y = jnp.dot(ordered, spread, preferred_element_type=F32)
        ids_y = jnp.where(keep, ids_y, 0.0)
        for g in range(NG):
            row = jnp.sum(ids_y[8 * g : 8 * g + 8, :], axis=0, keepdims=True)
            cl[y * NG + g] = jnp.broadcast_to(row, (8, 256))

    @pl.loop(0, 2 * NG)
    def _(k):
        y = jnp.where(k // NG == 0, y0, y1)
        rows = cl[y * NG + k % NG]
        for h in range(2):
            tile = jnp.broadcast_to(rows[0:1, 128 * h : 128 * h + 128], (128, 128))
            wide[pl.ds(pl.multiple_of(CS + k * 256 + h * 128, 8), 128), :] = tile.T

    wide[RA : RA + 2 * NG * GROUP, :] = jnp.full((2 * NG * GROUP, 128), -1.0, F32)
    colacc[...] = jnp.full(colacc.shape, -1.0, F32)

    @pl.loop(0, 3 * NG)
    def _(k):
        q[k // NG, k % NG, GROUP:256, :] = jnp.zeros((256 - GROUP, D), BF16)

    sub = lax.broadcasted_iota(jnp.int32, (128, 128), 0)
    low = idx_ref[...]
    low = jnp.where(low >= 0, low % 128, -1)
    for o in range(NS):
        rhs[:, 128 * o : 128 * o + 128] = (sub == low[o : o + 1, :]).astype(F32).astype(BF16)

    def group_of(n):
        return ((x - n // 2 + 4) % 4) * 2 + (z + n) % 2

    def ycopy(n, which):
        g = group_of(n)
        pos = first_pos if which == 0 else 2
        dev = rep_of(role - 1) if which == 0 else second_to
        return pltpu.make_async_remote_copy(
            src_ref=q.at[own_pos, g, pl.ds(0, GROUP)], dst_ref=q.at[pos, g, pl.ds(0, GROUP)],
            send_sem=ysend.at[which, n], recv_sem=yrecv.at[which, n],
            device_id={"rep": dev}, device_id_type=MESH,
        )

    def arrive(n):
        g = group_of(n)
        xs, zs = g // 2, g % 2

        @pl.loop(0, 8)
        def _(e):
            s = ((e // 2) * 2 + zs) * 8 + xs * 2 + e % 2

            @pl.when(s != me)
            def _():
                pltpu.make_async_remote_copy(
                    src_ref=outb.at[s], dst_ref=recv.at[s], send_sem=zsend.at[s], recv_sem=zrecv.at[s],
                    device_id={"shard": s}, device_id_type=MESH,
                ).wait_recv()

            @pl.when(s == me)
            def _():
                zlocal().wait()

            docs = recv[s].astype(F32)
            for i in range(PADDED):
                wide[pl.ds(STG + i * 64 + e, 8, stride=8), :] = docs[8 * i : 8 * i + 8, :]

        @pl.loop(0, GROUP // 16)
        def _(a):
            v = wide[pl.ds(pl.multiple_of(STG + a * 128, 8), 128), :]
            part = []
            for h in range(2):
                tiles = [v[64 * h + 8 * j : 64 * h + 8 * j + 8, :] for j in range(8)]
                square = tiles[0] * tiles[0]
                for j in range(1, 8):
                    square = square + tiles[j] * tiles[j]
                scale = lax.rsqrt(jnp.sum(square, axis=1, keepdims=True) + 1e-06)
                part.append([tile * scale for tile in tiles])
            for j in range(8):
                q[own_pos, g, pl.ds(pl.multiple_of(a * 16, 16), 16), 128 * j : 128 * j + 128] = jnp.concatenate(
                    [part[0][j], part[1][j]], axis=0
                ).astype(BF16)

        ycopy(n, 0).start()

        @pl.when(role >= 2)
        def _():
            ycopy(n, 1).start()

    away = lax.broadcasted_iota(jnp.int32, (GROUP, 256), 0) - lax.broadcasted_iota(jnp.int32, (GROUP, 256), 1)

    def tile(pa, ga, pb, gb, diagonal):
        g = lax.dot_general(q[pa, ga, 0:GROUP, :], q[pb, gb], LAST, preferred_element_type=F32)
        yb = jnp.where(pb == 0, y0, jnp.where(pb == 1, y1, y2))
        left = wide[pl.ds(pl.multiple_of(CS + (pa * NG + ga) * 256, 8), GROUP), :]
        right = cl[yb * NG + gb]
        at = pl.multiple_of(RA + (pa * NG + ga) * GROUP, 8)
        rows = wide[pl.ds(at, GROUP), :]
        for h in range(2):
            same = left.reshape(PADDED, 8, 128) == right[None, :, 128 * h : 128 * h + 128]
            if diagonal is not None:
                away_h = away[:, 128 * h : 128 * h + 128].reshape(PADDED, 8, 128)
                same = same & (away_h != jnp.where(diagonal, 0, 4096))
            vals = jnp.where(same, g[:, 128 * h : 128 * h + 128].reshape(PADDED, 8, 128), -1.0)
            rows = jnp.maximum(rows, vals.reshape(GROUP, 128))
            at_c = pb * NG + gb
            colacc[at_c, :, 128 * h : 128 * h + 128] = jnp.maximum(
                colacc[at_c, :, 128 * h : 128 * h + 128], jnp.max(vals, axis=0)
            )
        wide[pl.ds(at, GROUP), :] = rows

    def score(n):
        g = group_of(n)
        ycopy(n, 0).wait_recv()

        @pl.when(odd == 1)
        def _():
            ycopy(n, 1).wait_recv()

        @pl.loop(0, n)
        def _(m):
            gm = group_of(m)
            for v in range(4):
                ga = jnp.where((odd == 1) & (v >= 2), gm, g)
                gb = jnp.where((odd == 1) & (v >= 2), g, gm)
                pa = jnp.where(odd == 1, 0, v // 2)
                pb = jnp.where(odd == 1, 1 + v % 2, v % 2)
                tile(pa, ga, pb, gb, None)

        tile(0, g, 1, g, None)
        tile(0, g, jnp.where(odd == 1, 2, 0), g, odd == 0)

        @pl.when(odd == 0)
        def _():
            tile(1, g, 1, g, True)

    @pl.loop(0, NG + 1)
    def _(n):
        @pl.when(n < NG)
        def _():
            arrive(n)

        @pl.when(n > 0)
        def _():
            score(n - 1)

    spot8 = lax.broadcasted_iota(jnp.int32, (8, 256), 1) % 8 == lax.broadcasted_iota(jnp.int32, (8, 256), 0)
    out_lane = lax.broadcasted_iota(jnp.int32, (256, 128), 1) % 32
    gather = (lax.broadcasted_iota(jnp.int32, (256, 128), 0) // 8 == out_lane).astype(F32).astype(BF16)
    lane8 = lax.broadcasted_iota(jnp.int32, (8, 128), 1)
    tsrc[...] = jnp.full(tsrc.shape, -1.0, F32)

    @pl.loop(0, 3)
    def _(p):
        yp = jnp.where(p == 0, y0, jnp.where(p == 1, y1, y2))
        parts = ([], [], [])
        for g in range(NG):
            col = jnp.max(colacc[p * NG + g], axis=0, keepdims=True)
            for part, kept in zip(parts, pieces(col)):
                part.append(jnp.where(spot8, kept, 0.0).astype(BF16).astype(F32))
        best = 0.0
        for part in parts:
            left = jnp.concatenate(part, axis=0).astype(BF16)
            best = best + jnp.dot(left, gather, preferred_element_type=F32)
        mine = lax.broadcasted_iota(jnp.int32, (NS, 128), 1) // 32 == yp
        tsrc[...] = jnp.maximum(tsrc[...], jnp.where(mine, best, -1.0))

    @pl.loop(0, 2 * NG)
    def _(k):
        yp = jnp.where(k // NG == 0, y0, y1)
        rows = wide[pl.ds(pl.multiple_of(RA + k * GROUP, 8), GROUP), :].reshape(PADDED, 8, 128)
        rows = jnp.max(rows, axis=2, keepdims=True)
        best = jnp.full((8, 128), -1.0, F32)
        for i in range(PADDED):
            best = jnp.where(lane8 % 32 == i, rows[i], best)
        at = pl.ds(pl.multiple_of((k % NG) * 8, 8), 8)
        tsrc[at, :] = jnp.maximum(tsrc[at, :], jnp.where(lane8 // 32 == yp, best, -1.0))

    def r1(k):
        dev = (rep + k) % NR
        return pltpu.make_async_remote_copy(
            src_ref=tsrc, dst_ref=trecv.at[k], send_sem=r1send.at[k], recv_sem=r1recv.at[k],
            device_id={"rep": dev}, device_id_type=MESH,
        )

    for k in range(1, NR):
        r1(k).start()
    for k in range(1, NR):
        r1(k).wait_recv()
    full = jnp.maximum(jnp.maximum(tsrc[...], trecv[1]), jnp.maximum(trecv[2], trecv[3]))
    for r in range(NS):
        trow[r] = full[r : r + 1, :]

    def slot_of(s):
        zz, xx, cc = s // 8, (s // 2) % 4, s % 2
        return (xx * 2 + zz % 2) * 8 + (zz // 2) * 2 + cc

    def r2(s):
        return pltpu.make_async_remote_copy(
            src_ref=trow.at[slot_of(s)], dst_ref=vrecv.at[me], send_sem=r2send.at[s], recv_sem=r2recv.at[me],
            device_id={"shard": s}, device_id_type=MESH,
        )

    @pl.loop(1, NS)
    def _(k):
        r2((me + k) % NS).start()

    vrecv[me] = trow[slot_of(me)]

    @pl.loop(1, NS)
    def _(k):
        s = (me + k) % NS
        pltpu.make_async_remote_copy(
            src_ref=trow.at[slot_of(s)], dst_ref=vrecv.at[s], send_sem=r2send.at[s], recv_sem=r2recv.at[s],
            device_id={"shard": s}, device_id_type=MESH,
        ).wait_recv()

    sub64 = lax.broadcasted_iota(jnp.int32, (64, 128), 0)
    high = idx_ref[...]
    high = jnp.where(high >= 0, high // 128, -1)
    for o in range(NS):
        hit = sub64 == high[o : o + 1, :]
        for w, kept in enumerate(pieces(vrecv[o])):
            lhs[64 * w : 64 * w + 64, 128 * o : 128 * o + 128] = jnp.where(hit, kept, 0.0).astype(BF16)
    done = lax.dot_general(lhs[...], rhs[...], LAST, preferred_element_type=F32)
    done = done[0:64, :] + done[64:128, :] + done[128:192, :]
    out_ref[...] = done[0 : DOCS // 128, :]

    @pl.loop(1, NS)
    def _(k):
        s = (me + k) % NS
        zcopy(s).wait_send()
        r2(s).wait_send()

    for k in range(1, NR):
        r1(k).wait_send()

    @pl.loop(0, NG)
    def _(n):
        ycopy(n, 0).wait_send()

        @pl.when(role >= 2)
        def _():
            ycopy(n, 1).wait_send()


def shards(embeddings, send_index, place_index, slot_cluster, pair_list):
    def lanes(a):
        a = a.reshape(NS, NR, PART)
        return jnp.pad(a, ((0, 0), (0, 0), (0, 32 - PART)), constant_values=-1).reshape(NS, 128)

    vm = pl.BlockSpec(memory_space=pltpu.VMEM)
    sm = pl.BlockSpec(memory_space=pltpu.SMEM)
    dma = pltpu.SemaphoreType.DMA
    out = pl.pallas_call(
        kernel,
        out_shape=jax.ShapeDtypeStruct((DOCS // 128, 128), F32),
        in_specs=[sm, sm, pl.BlockSpec(memory_space=pl.ANY), vm, vm],
        out_specs=vm,
        scratch_shapes=[
            pltpu.VMEM((DOCS * 8, 128), F32),
            pltpu.VMEM((3, NG, 256, D), BF16),
            pltpu.VMEM((NS, MSG, 128), BF16),
            pltpu.VMEM((NS, MSG, 128), BF16),
            pltpu.VMEM((2, CHUNK, D), BF16),
            pltpu.VMEM((3 * NG, 8, 256), F32),
            pltpu.VMEM((NR * NG, 8, 256), F32),
            pltpu.VMEM((NS, 128), F32),
            pltpu.VMEM((192, NS * 128), BF16),
            pltpu.VMEM((128, NS * 128), BF16),
            pltpu.VMEM((NS, 128), F32),
            pltpu.VMEM((NR, NS, 128), F32),
            pltpu.VMEM((NS, 1, 128), F32),
            pltpu.VMEM((NS, 1, 128), F32),
            dma((2,)),
            dma((NS,)),
            dma((NS,)),
            dma((2, NG)),
            dma((2, NG)),
            dma((NR,)),
            dma((NR,)),
            dma((NS,)),
            dma((NS,)),
        ],
        compiler_params=pltpu.CompilerParams(
            collective_id=0, has_side_effects=True, vmem_limit_bytes=60 * 1024 * 1024
        ),
        name="dedup",
    )(send_index, slot_cluster, embeddings, lanes(send_index), lanes(place_index))
    return out.reshape(-1)


def solution(mesh):
    return jax.shard_map(
        shards,
        mesh=mesh,
        in_specs=(P("shard", None), P("shard"), P("shard"), P("shard"), P(("shard", "rep"), None)),
        out_specs=P("shard"),
        check_vma=False,
    )
```

time: 804 us -> 150 us (0.19)
  local copies, waits for them, and re-layouts: 348 us -> 4.93 us
  waiting for transfers between devices: 297 us -> 0 us
  Pallas kernels: 0 us -> 144 us
  matrix products: 68.8 us -> 0 us
  blocking collectives: 37.6 us -> 0 us
  other arithmetic: 36.4 us -> 0 us
  starting transfers between devices: 13.3 us -> 0 us
    all_to_all x1 -> x0, waiting for transfers between devices: 297 us -> none  [shards(): lax.all_to_all(outgoing, 'shard', split_axis=0, concat_axis=0, tiled=True)]
    gather x46 -> x0, local copies, waits for them, and re-layouts: 249 us -> none  [the longest x11 84.6 us: visit(): blocks[second]]
    pallas_call x0 -> x1, Pallas kernels: none -> 144 us  [shards(): pl.pallas_call(kernel, out_shape=jax.ShapeDtypeStruct((DOCS // 128, 128),...]
    dot_general x11 -> x0, matrix products: 68.8 us -> none  [visit(): jnp.einsum('pad,pbd->pab', blocks[first], blocks[second], preferred_eleme...]
    scatter x2 -> x0, local copies, waits for them, and re-layouts: 65.7 us -> none  [the longest x1 41.2 us: shards(): jnp.zeros((blocks_held * BLK, D), jnp.bfloat16).at[place_index]]
    reshape x6 -> x4, local copies, waits for them, and re-layouts: 32.4 us -> 3.33 us  [the longest x2 1.96 us: lanes(): a = a.reshape(NS, NR, PART)]
    all_to_all x1 -> x0, blocking collectives: 24 us -> none  [shards(): lax.all_to_all(outbound, 'shard', split_axis=0, concat_axis=0, tiled=True)]
    another operation x22 -> x0, other arithmetic: 15.3 us -> none  [the longest x11 7.63 us: visit(): best = best.at[first].max(jnp.max(values, axis=2))]
  transfers between devices with their start and end apart: 1 -> 0, of which waited for: 1 -> 0; matrix products, arithmetic and copies ran while one was open for 0% -> 0% of each run, Pallas kernels for 0% -> 0%
where the time goes in v1:
time: 150 us; the launch traced here: 149 us
  Pallas kernels  144 us (96%)
  local copies, waits for them, and re-layouts  4.93 us (3%)
    pallas_call x1, Pallas kernels, shards(): pl.pallas_call(kernel, out_shape=jax.ShapeDtypeStruct((DOCS // 128, 128),...  144 us

profile of v1, /device:TPU:1, one launch (start us, length us, event | category | flops | bytes accessed | tf_op | source)
XLA Modules:
  0.0 148.9 jit_solution(11906337072380791989)
XLA Ops:
  0.0 1.0 reshape.17
  1.0 0.1 copy.10
  1.1 0.7 copy.8.place_ref
  1.8 1.0 reshape.15
  2.8 0.1 copy.9
  2.9 0.7 copy.7.idx_ref
  3.6 144.0 %dedup.1 = f32[50,128]{1,0:T(8,128)} custom-call(s32[6400]{0:T(1024)} %send_ref.1, s32[6656]{0:T(1024)} %table_ref.1, bf16[6400,1024]{1,0:T(8,128)(2,1)} %emb_ref.1, s32[64,128]{1,0:T(8,128)} %copy.7.idx_ref, s32[64,128]{1,0:T(8,128)} %copy.8.place_ref), custom_call_target="tpu_custom_call" | custom-call | tf_op jit(solution)/shard_map/dedup/pallas_call | solution.py:400
  147.6 1.4 copy.12
  (2 shorter events, 0.0 us)

commit v2 on v1

v2 whole, which is shorter than its diff:
```python
import functools

import jax
import jax.numpy as jnp
from jax import lax
from jax.experimental import pallas as pl
from jax.experimental.pallas import tpu as pltpu
from jax.sharding import PartitionSpec as P

D = 1024
BLK = 256
DOCS = 6400
NS = 64
NR = 4
SHARE = 100
PART = 25
PADDED = 26
MSG = PADDED * 8
GROUP = PADDED * 8
NG = 8
CHUNK = 400
NCHUNK = DOCS // CHUNK
NBUF = 8
FLAT = DOCS // 128
MESH = pl.DeviceIdType.MESH
F32 = jnp.float32
BF16 = jnp.bfloat16
LAST = (((1,), (1,)), ((), ()))


def pieces(v):
    a = v.astype(BF16).astype(F32)
    r = v - a
    b = r.astype(BF16).astype(F32)
    return a, b, r - b


def kernel(
    send_hbm, table_hbm, emb_ref, idx_hbm, place_hbm, out_ref,
    send_ref, table_ref, idx_ref, place_ref,
    wide, q, outb, recv, emb, stage, cs, ra, colacc, cl, ctmp, tsrc, trecv, trow, vrecv, res,
    isem, bsem, esem, zsend, zrecv, ysend, yrecv, r1send, r1recv, r2send, r2recv, r3send, r3recv,
):
    me = lax.axis_index("shard")
    rep = lax.axis_index("rep")
    z, x, c = me // 8, (me // 2) % 4, me % 2
    def rep_of(r):
        return (r + 2 * c) % 4

    def pick(a, b, c_, d):
        return jnp.where(role == 0, a, jnp.where(role == 1, b, jnp.where(role == 2, c_, d)))

    role = rep_of(rep)
    y0 = rep
    y1 = rep_of(pick(3, 0, 1, 3))
    y2 = rep_of(pick(0, 2, 3, 0))

    def fetch(ch, slot):
        return pltpu.make_async_copy(
            emb_ref.at[pl.ds(pl.multiple_of(ch * CHUNK, 16), CHUNK)], emb.at[slot], esem.at[slot]
        )

    ints = [
        pltpu.make_async_copy(a, b, isem.at[i])
        for i, (a, b) in enumerate(
            [(send_hbm, send_ref), (table_hbm, table_ref), (idx_hbm, idx_ref), (place_hbm, place_ref)]
        )
    ]
    for i in range(NBUF):
        fetch(i, i).start()
    for copy in ints:
        copy.start()

    def in_line(k):
        return {"shard": ((z + k) % 8) * 8 + x * 2 + c}

    def in_plane(k):
        return {"shard": z * 8 + (x * 2 + c + k) % 8}

    barrier = pltpu.get_barrier_semaphore()
    for k in range(1, NR):
        pl.semaphore_signal(barrier, inc=1, device_id={"rep": (rep + k) % NR}, device_id_type=MESH)
    for k in range(1, 8):
        pl.semaphore_signal(barrier, inc=1, device_id=in_plane(k), device_id_type=MESH)
        pl.semaphore_signal(barrier, inc=1, device_id=in_line(k), device_id_type=MESH)

    @pl.loop(0, NCHUNK)
    def _(ch):
        slot = ch % NBUF
        fetch(ch, slot).wait()

        @pl.loop(0, CHUNK // 16, unroll=5)
        def _(r):
            rows = emb[slot, pl.ds(pl.multiple_of(r * 16, 16), 16), :].astype(F32)
            base = ch * (CHUNK * 8) + r * 128
            for h in range(2):
                for j in range(8):
                    wide[pl.ds(pl.multiple_of(base + h * 64 + j * 8, 8), 8), :] = rows[
                        8 * h : 8 * h + 8, 128 * j : 128 * j + 128
                    ]

        @pl.when(ch + NBUF < NCHUNK)
        def _():
            fetch(ch + NBUF, slot).start()

        @pl.when(ch == NCHUNK // 2)
        def _():
            pl.semaphore_wait(barrier, 14 + NR - 1)
            for k in range(1, 8):
                pl.semaphore_signal(bsem, inc=1, device_id=in_plane(k), device_id_type=MESH)

    for copy in ints:
        copy.wait()
    pl.semaphore_wait(bsem, 7)

    def zcopy(dst):
        return pltpu.make_async_remote_copy(
            src_ref=outb.at[dst], dst_ref=recv.at[me], send_sem=zsend.at[dst], recv_sem=zrecv.at[me],
            device_id={"shard": dst}, device_id_type=MESH,
        )

    def zlocal():
        return pltpu.make_async_copy(outb.at[me], recv.at[me], zrecv.at[me])

    def address(i):
        return (i // 8) * 64 + i % 8

    def send(k):
        n = k // 8
        t, h, w, b = n // 2, n % 2, (k // 2) % 4, k % 2
        dst = ((z + h + 2 * w) % 8) * 8 + ((x + t) % 4) * 2 + (c + b) % 2
        base = dst * SHARE + rep * PART
        for a in range(PADDED // 2):
            i0 = send_ref[base + 2 * a]
            i1 = send_ref[base + min(2 * a + 1, PART - 1)]
            v0 = wide[pl.ds(address(i0), 8, stride=8), :]
            v1 = wide[pl.ds(address(i1), 8, stride=8), :]
            outb[dst, pl.ds(16 * a, 16), :] = jnp.concatenate([v0, v1], axis=0).astype(BF16)

        @pl.when(dst != me)
        def _():
            zcopy(dst).start()

        @pl.when(dst == me)
        def _():
            zlocal().start()

    @pl.loop(0, NS)
    def _(k):
        send(k)

    lane1 = lax.broadcasted_iota(jnp.int32, (1, 128), 1)

    def share_of(flat, o):
        a, off = o * SHARE // 128, o * SHARE % 128
        b = min(a + 1, FLAT - 1)
        both = jnp.where(lane1 >= off, flat[a : a + 1, :], flat[b : b + 1, :])
        both = both if off == 0 else pltpu.roll(both, 128 - off, 1)
        return jnp.where(lane1 < SHARE, both, -1)

    for g in range(NG):
        for e in range(8):
            s = ((e // 2) * 2 + g % 2) * 8 + (g // 2) * 2 + e % 2
            ctmp[8 * g + e : 8 * g + e + 1, :] = share_of(place_ref, s)
    block = ctmp[...] // BLK
    ids = jnp.full((NS, 128), -1.0, F32)
    for b in range(table_ref.shape[0] // BLK):
        ids = jnp.where(block == b, (table_ref[b * BLK] - me * 26).astype(F32), ids)
    ordered = ids.astype(BF16)
    lane = lax.broadcasted_iota(jnp.int32, (128, 256), 0)
    spot = lax.broadcasted_iota(jnp.int32, (128, 256), 1)
    keep = (lax.broadcasted_iota(jnp.int32, (NS, 256), 1) % 8) == (
        lax.broadcasted_iota(jnp.int32, (NS, 256), 0) % 8
    )
    for y in range(NR):
        spread = ((lane == PART * y + spot // 8) & (spot < 8 * PART)).astype(F32).astype(BF16)
        ids_y = jnp.dot(ordered, spread, preferred_element_type=F32)
        ids_y = jnp.where(keep, ids_y, 0.0)
        for g in range(NG):
            row = jnp.sum(ids_y[8 * g : 8 * g + 8, :], axis=0, keepdims=True)
            cl[y * NG + g] = jnp.broadcast_to(jnp.where(spot[0:1, :] < 8 * PART, row, -1.0), (8, 256))

    @pl.loop(0, 2 * NG)
    def _(k):
        y = jnp.where(k // NG == 0, y0, y1)
        rows = cl[y * NG + k % NG]
        for h in range(2):
            tile = jnp.broadcast_to(rows[0:1, 128 * h : 128 * h + 128], (128, 128))
            cs[pl.ds(pl.multiple_of(k * 256 + h * 128, 8), 128), :] = tile.T

    ra[...] = jnp.full(ra.shape, -1.0, F32)
    colacc[...] = jnp.full(colacc.shape, -1.0, F32)

    @pl.loop(0, 3 * NG)
    def _(k):
        q[k // NG, k % NG, GROUP:256, :] = jnp.zeros((256 - GROUP, D), BF16)

    sub = lax.broadcasted_iota(jnp.int32, (128, 128), 0)
    for o in range(NS):
        low = share_of(idx_ref, o)
        ctmp[o : o + 1, :] = low
        low = jnp.where(low >= 0, low % 128, -1)
        emb[o // 8, 192:320, 128 * (o % 8) : 128 * (o % 8) + 128] = (sub == low).astype(F32).astype(BF16)

    def group_of(n):
        return ((x - n // 2 + 4) % 4) * 2 + (z + n) % 2

    def ycopy(n, which):
        g = group_of(n)
        at = jnp.where(role >= 2, 1, 0) if which == 0 else 0
        dev = rep_of(pick(1, 2, 1, 2)) if which == 0 else rep_of(0)
        return pltpu.make_async_remote_copy(
            src_ref=q.at[0, g, pl.ds(0, GROUP)], dst_ref=q.at[1 + at, g, pl.ds(0, GROUP)],
            send_sem=ysend.at[which, n], recv_sem=yrecv.at[at, n],
            device_id={"rep": dev}, device_id_type=MESH,
        )

    def ywait(n, at):
        g = group_of(n)
        pltpu.make_async_remote_copy(
            src_ref=q.at[0, g, pl.ds(0, GROUP)], dst_ref=q.at[1 + at, g, pl.ds(0, GROUP)],
            send_sem=ysend.at[0, n], recv_sem=yrecv.at[at, n],
            device_id={"rep": rep_of(pick(1, 2, 1, 2))}, device_id_type=MESH,
        ).wait_recv()

    def arrive(n):
        g = group_of(n)
        xs, zs = g // 2, g % 2

        @pl.loop(0, 8)
        def _(e):
            s = ((e // 2) * 2 + zs) * 8 + xs * 2 + e % 2

            @pl.when(s != me)
            def _():
                pltpu.make_async_remote_copy(
                    src_ref=outb.at[s], dst_ref=recv.at[s], send_sem=zsend.at[s], recv_sem=zrecv.at[s],
                    device_id={"shard": s}, device_id_type=MESH,
                ).wait_recv()

            @pl.when(s == me)
            def _():
                zlocal().wait()

            docs = recv[s].astype(F32)
            for i in range(PADDED):
                stage[pl.ds(i * 64 + e, 8, stride=8), :] = docs[8 * i : 8 * i + 8, :]

        @pl.loop(0, GROUP // 16)
        def _(a):
            v = stage[pl.ds(pl.multiple_of(a * 128, 8), 128), :]
            part = []
            for h in range(2):
                tiles = [v[64 * h + 8 * j : 64 * h + 8 * j + 8, :] for j in range(8)]
                square = tiles[0] * tiles[0]
                for j in range(1, 8):
                    square = square + tiles[j] * tiles[j]
                scale = lax.rsqrt(jnp.sum(square, axis=1, keepdims=True) + 1e-06)
                part.append([tile * scale for tile in tiles])
            for j in range(8):
                q[0, g, pl.ds(pl.multiple_of(a * 16, 16), 16), 128 * j : 128 * j + 128] = jnp.concatenate(
                    [part[0][j], part[1][j]], axis=0
                ).astype(BF16)

        ycopy(n, 0).start()

        @pl.when(role == 3)
        def _():
            ycopy(n, 1).start()

    away = lax.broadcasted_iota(jnp.int32, (GROUP, 256), 0) - lax.broadcasted_iota(jnp.int32, (GROUP, 256), 1)

    def tile(pa, ga, pb, gb, diagonal):
        g = lax.dot_general(q[pa, ga, 0:GROUP, :], q[pb, gb], LAST, preferred_element_type=F32)
        yb = jnp.where(pb == 0, y0, jnp.where(pb == 1, y1, y2))
        left = cs[pl.ds(pl.multiple_of((pa * NG + ga) * 256, 8), GROUP), :]
        right = cl[yb * NG + gb]
        at = pl.multiple_of((pa * NG + ga) * GROUP, 8)
        rows = ra[pl.ds(at, GROUP), :]
        for h in range(2):
            same = left.reshape(PADDED, 8, 128) == right[None, :, 128 * h : 128 * h + 128]
            if diagonal is not None:
                away_h = away[:, 128 * h : 128 * h + 128].reshape(PADDED, 8, 128)
                same = same & (away_h != jnp.where(diagonal, 0, 4096))
            vals = jnp.where(same, g[:, 128 * h : 128 * h + 128].reshape(PADDED, 8, 128), -1.0)
            rows = jnp.maximum(rows, vals.reshape(GROUP, 128))
            at_c = pb * NG + gb
            colacc[at_c, :, 128 * h : 128 * h + 128] = jnp.maximum(
                colacc[at_c, :, 128 * h : 128 * h + 128], jnp.max(vals, axis=0)
            )
        ra[pl.ds(at, GROUP), :] = rows

    def before(n):
        g = group_of(n)

        @pl.when(role != 3)
        def _():
            @pl.loop(0, n)
            def _(m):
                gm = group_of(m)
                tile(0, g, jnp.where(role == 2, 2, 1), gm, None)
                tile(0, g, jnp.where(role == 1, 2, 0), gm, None)

        @pl.when(role == 3)
        def _():
            @pl.loop(0, n)
            def _(m):
                tile(0, g, 0, group_of(m), None)

        @pl.when(role != 1)
        def _():
            tile(0, g, 0, g, True)

    def after(n):
        g = group_of(n)

        @pl.when(role != 3)
        def _():
            ywait(n, 0)

        @pl.when(role == 0)
        def _():
            @pl.loop(0, n + 1)
            def _(m):
                tile(0, group_of(m), 1, g, None)

        @pl.when((role == 1) | (role == 2))
        def _():
            ywait(n, 1)

            @pl.loop(0, n)
            def _(m):
                gm = group_of(m)
                tile(0, gm, 2, g, None)
                tile(1, g, 2, gm, None)
                tile(1, gm, 2, g, None)
                tile(jnp.where(role == 1, 0, 1), gm, 1, g, None)

            tile(0, g, 2, g, None)
            tile(1, g, 2, g, None)
            tile(jnp.where(role == 1, 0, 1), g, 1, g, role == 2)

    @pl.loop(0, NG + 1)
    def _(n):
        @pl.when(n < NG)
        def _():
            arrive(n)

        @pl.when(n > 0)
        def _():
            after(n - 1)

        @pl.when(n < NG)
        def _():
            before(n)

    spot8 = lax.broadcasted_iota(jnp.int32, (8, 256), 1) % 8 == lax.broadcasted_iota(jnp.int32, (8, 256), 0)
    out_lane = lax.broadcasted_iota(jnp.int32, (256, 128), 1) % PART
    gather = (lax.broadcasted_iota(jnp.int32, (256, 128), 0) // 8 == out_lane).astype(F32).astype(BF16)
    lane8 = lax.broadcasted_iota(jnp.int32, (8, 128), 1)
    tsrc[...] = jnp.full(tsrc.shape, -1.0, F32)

    @pl.loop(0, 3)
    def _(p):
        yp = jnp.where(p == 0, y0, jnp.where(p == 1, y1, y2))
        parts = ([], [], [])
        for g in range(NG):
            col = jnp.max(colacc[p * NG + g], axis=0, keepdims=True)
            for part, kept in zip(parts, pieces(col)):
                part.append(jnp.where(spot8, kept, 0.0).astype(BF16).astype(F32))
        best = 0.0
        for part in parts:
            left = jnp.concatenate(part, axis=0).astype(BF16)
            best = best + jnp.dot(left, gather, preferred_element_type=F32)
        mine = lax.broadcasted_iota(jnp.int32, (NS, 128), 1) // PART == yp
        tsrc[...] = jnp.maximum(tsrc[...], jnp.where(mine, best, -1.0))

    @pl.loop(0, 2 * NG)
    def _(k):
        yp = jnp.where(k // NG == 0, y0, y1)
        rows = ra[pl.ds(pl.multiple_of(k * GROUP, 8), GROUP), :].reshape(PADDED, 8, 128)
        rows = jnp.max(rows, axis=2, keepdims=True)
        best = jnp.full((8, 128), -1.0, F32)
        for i in range(PART):
            best = jnp.where(lane8 % PART == i, rows[i], best)
        at = pl.ds(pl.multiple_of((k % NG) * 8, 8), 8)
        tsrc[at, :] = jnp.maximum(tsrc[at, :], jnp.where(lane8 // PART == yp, best, -1.0))

    def r1(k):
        dev = (rep + k) % NR
        return pltpu.make_async_remote_copy(
            src_ref=tsrc.at[pl.ds(pl.multiple_of(dev * 16, 16), 16)], dst_ref=trecv.at[k],
            send_sem=r1send.at[k], recv_sem=r1recv.at[k], device_id={"rep": dev}, device_id_type=MESH,
        )

    for k in range(1, NR):
        r1(k).start()

    @pl.loop(1, NS)
    def _(k):
        zcopy((me + k) % NS).wait_send()

    @pl.loop(0, NG)
    def _(n):
        ycopy(n, 0).wait_send()

        @pl.when(role == 3)
        def _():
            ycopy(n, 1).wait_send()

    for k in range(1, NR):
        r1(k).wait_recv()
    full = tsrc[pl.ds(pl.multiple_of(rep * 16, 16), 16), :]
    full = jnp.maximum(jnp.maximum(full, trecv[1]), jnp.maximum(trecv[2], trecv[3]))
    for r in range(16):
        trow[r] = full[r : r + 1, :]

    def source(r):
        e, g = r % 8, 2 * rep + r // 8
        return ((e // 2) * 2 + g % 2) * 8 + (g // 2) * 2 + e % 2

    def r2(r):
        return pltpu.make_async_remote_copy(
            src_ref=trow.at[r], dst_ref=vrecv.at[me], send_sem=r2send.at[r], recv_sem=r2recv.at[me],
            device_id={"shard": source(r)}, device_id_type=MESH,
        )

    @pl.loop(0, 16)
    def _(r):
        @pl.when(source(r) != me)
        def _():
            r2(r).start()

        @pl.when(source(r) == me)
        def _():
            vrecv[me] = trow[r]

    def r3(k):
        return pltpu.make_async_remote_copy(
            src_ref=res, dst_ref=res, send_sem=r3send.at[k], recv_sem=r3recv,
            device_id={"rep": (rep + k) % NR}, device_id_type=MESH,
        )

    @pl.when(x == rep)
    def _():
        @pl.loop(1, NS)
        def _(k):
            s = (me + k) % NS
            pltpu.make_async_remote_copy(
                src_ref=trow.at[0], dst_ref=vrecv.at[s], send_sem=r2send.at[0], recv_sem=r2recv.at[s],
                device_id={"shard": s}, device_id_type=MESH,
            ).wait_recv()

        sub64 = lax.broadcasted_iota(jnp.int32, (64, 128), 0)
        high = ctmp[...]
        high = jnp.where(high >= 0, high // 128, -1)
        for o in range(NS):
            hit = sub64 == high[o : o + 1, :]
            for w, kept in enumerate(pieces(vrecv[o])):
                emb[o // 8, 64 * w : 64 * w + 64, 128 * (o % 8) : 128 * (o % 8) + 128] = jnp.where(
                    hit, kept, 0.0
                ).astype(BF16)
        done = 0.0
        for j in range(8):
            done = done + lax.dot_general(
                emb[j, 0:192, :], emb[j, 192:320, :], LAST, preferred_element_type=F32
            )
        res[...] = (done[0:64, :] + done[64:128, :] + done[128:192, :])[0:56, :]
        for k in range(1, NR):
            r3(k).start()
        for k in range(1, NR):
            r3(k).wait_send()

    @pl.when(x != rep)
    def _():
        r3(1).wait_recv()

    out_ref[...] = res[0:FLAT, :]

    @pl.loop(0, 16)
    def _(r):
        @pl.when(source(r) != me)
        def _():
            r2(r).wait_send()

    for k in range(1, NR):
        r1(k).wait_send()


def shards(embeddings, send_index, place_index, slot_cluster, pair_list):
    vm = pl.BlockSpec(memory_space=pltpu.VMEM)
    hbm = pl.BlockSpec(memory_space=pl.ANY)
    dma = pltpu.SemaphoreType.DMA
    out = pl.pallas_call(
        kernel,
        out_shape=jax.ShapeDtypeStruct((DOCS // 128, 128), F32),
        in_specs=[hbm] * 5,
        out_specs=vm,
        scratch_shapes=[
            pltpu.SMEM((DOCS,), jnp.int32),
            pltpu.SMEM(slot_cluster.shape, jnp.int32),
            pltpu.VMEM((FLAT, 128), jnp.int32),
            pltpu.VMEM((FLAT, 128), jnp.int32),
            pltpu.VMEM((DOCS * 8, 128), F32),
            pltpu.VMEM((3, NG, 256, D), BF16),
            pltpu.VMEM((NS, MSG, 128), BF16),
            pltpu.VMEM((NS, MSG, 128), BF16),
            pltpu.VMEM((NBUF, CHUNK, D), BF16),
            pltpu.VMEM((GROUP * 8, 128), F32),
            pltpu.VMEM((2 * NG * 256, 128), F32),
            pltpu.VMEM((2 * NG * GROUP, 128), F32),
            pltpu.VMEM((3 * NG, 8, 256), F32),
            pltpu.VMEM((NR * NG, 8, 256), F32),
            pltpu.VMEM((NS, 128), jnp.int32),
            pltpu.VMEM((NS, 128), F32),
            pltpu.VMEM((NR, 16, 128), F32),
            pltpu.VMEM((16, 1, 128), F32),
            pltpu.VMEM((NS, 1, 128), F32),
            pltpu.VMEM((56, 128), F32),
            dma((4,)),
            pltpu.SemaphoreType.REGULAR,
            dma((NBUF,)),
            dma((NS,)),
            dma((NS,)),
            dma((2, NG)),
            dma((2, NG)),
            dma((NR,)),
            dma((NR,)),
            dma((16,)),
            dma((NS,)),
            dma((NR,)),
            dma(()),
        ],
        compiler_params=pltpu.CompilerParams(
            collective_id=0, has_side_effects=True, vmem_limit_bytes=62 * 1024 * 1024
        ),
        name="dedup",
    )(
        send_index, slot_cluster, embeddings, send_index.reshape(FLAT, 128), place_index.reshape(FLAT, 128)
    )
    return out.reshape(-1)


def solution(mesh):
    return jax.shard_map(
        shards,
        mesh=mesh,
        in_specs=(P("shard", None), P("shard"), P("shard"), P("shard"), P(("shard", "rep"), None)),
        out_specs=P("shard"),
        check_vma=False,
    )
```

time: 150 us -> 141 us (0.940)
  Pallas kernels: 144 us -> 139 us
  local copies, waits for them, and re-layouts: 4.93 us -> 1.36 us
    pallas_call x1, Pallas kernels: 144 us -> 139 us  [shards(): pl.pallas_call(kernel, out_shape=jax.ShapeDtypeStruct((DOCS // 128, 128),...]
    reshape x4 -> x0, local copies, waits for them, and re-layouts: 3.33 us -> none  [the longest x2 1.96 us: lanes(): a = a.reshape(NS, NR, PART)]
where the time goes in v2:
time: 141 us; the launch traced here: 140 us
  Pallas kernels  139 us (99%)
    pallas_call x1, Pallas kernels, shards(): pl.pallas_call(kernel, out_shape=jax.ShapeDtypeStruct((DOCS // 128, 128),...  139 us

profile of v2, /device:TPU:1, one launch (start us, length us, event | category | flops | bytes accessed | tf_op | source)
XLA Modules:
  0.0 140.4 jit_solution(15444041186978277340)
XLA Ops:
  0.0 139.0 %dedup.1 = f32[50,128]{1,0:T(8,128)} custom-call(s32[6400]{0:T(1024)} %send_hbm.1, s32[6656]{0:T(1024)} %table_hbm.1, bf16[6400,1024]{1,0:T(8,128)(2,1)} %emb_ref.1, s32[50,128]{1,0:T(8,128)} %bitcast.4, s32[50,128]{1,0:T(8,128)} %bitcast.5), custom_call_target="tpu_custom_call" | custom-call | tf_op jit(solution)/shard_map/dedup/pallas_call | solution.py:494
  139.0 1.4 copy.6

commit v3 on v2

--- a/solution.py
+++ b/solution.py
@@ -66,23 +66,25 @@
             [(send_hbm, send_ref), (table_hbm, table_ref), (idx_hbm, idx_ref), (place_hbm, place_ref)]
         )
     ]
+    def in_line(k):
+        other = (z * 2 + c + k) % 16
+        return {"shard": (other // 2) * 8 + x * 2 + other % 2}
+
+    def in_ring(k):
+        return {"shard": z * 8 + ((x + k) % 4) * 2 + c}
+
+    barrier = pltpu.get_barrier_semaphore()
+    for k in range(1, NR):
+        pl.semaphore_signal(barrier, inc=1, device_id={"rep": (rep + k) % NR}, device_id_type=MESH)
+    for k in range(1, 4):
+        pl.semaphore_signal(barrier, inc=1, device_id=in_ring(k), device_id_type=MESH)
+    for k in range(1, 16):
+        pl.semaphore_signal(barrier, inc=1, device_id=in_line(k), device_id_type=MESH)
+
     for i in range(NBUF):
         fetch(i, i).start()
     for copy in ints:
         copy.start()
-
-    def in_line(k):
-        return {"shard": ((z + k) % 8) * 8 + x * 2 + c}
-
-    def in_plane(k):
-        return {"shard": z * 8 + (x * 2 + c + k) % 8}
-
-    barrier = pltpu.get_barrier_semaphore()
-    for k in range(1, NR):
-        pl.semaphore_signal(barrier, inc=1, device_id={"rep": (rep + k) % NR}, device_id_type=MESH)
-    for k in range(1, 8):
-        pl.semaphore_signal(barrier, inc=1, device_id=in_plane(k), device_id_type=MESH)
-        pl.semaphore_signal(barrier, inc=1, device_id=in_line(k), device_id_type=MESH)
 
     @pl.loop(0, NCHUNK)
     def _(ch):
@@ -103,15 +105,11 @@
         def _():
             fetch(ch + NBUF, slot).start()
 
-        @pl.when(ch == NCHUNK // 2)
-        def _():
-            pl.semaphore_wait(barrier, 14 + NR - 1)
-            for k in range(1, 8):
-                pl.semaphore_signal(bsem, inc=1, device_id=in_plane(k), device_id_type=MESH)
-
     for copy in ints:
         copy.wait()
-    pl.semaphore_wait(bsem, 7)
+    pl.semaphore_wait(barrier, 15 + 3 + NR - 1)
+    for k in range(1, 4):
+        pl.semaphore_signal(bsem, inc=1, device_id=in_ring(k), device_id_type=MESH)
 
     def zcopy(dst):
         return pltpu.make_async_remote_copy(
@@ -145,7 +143,13 @@
         def _():
             zlocal().start()
 
-    @pl.loop(0, NS)
+    @pl.loop(0, 16)
+    def _(k):
+        send(k)
+
+    pl.semaphore_wait(bsem, 3)
+
+    @pl.loop(16, NS)
     def _(k):
         send(k)
 
@@ -262,11 +266,11 @@
                     [part[0][j], part[1][j]], axis=0
                 ).astype(BF16)
 
+        @pl.when(role == 3)
+        def _():
+            ycopy(n, 1).start()
+
         ycopy(n, 0).start()
-
-        @pl.when(role == 3)
-        def _():
-            ycopy(n, 1).start()
 
     away = lax.broadcasted_iota(jnp.int32, (GROUP, 256), 0) - lax.broadcasted_iota(jnp.int32, (GROUP, 256), 1)
 

time: 141 us -> 137 us (0.972)
  Pallas kernels: 139 us -> 134 us
    pallas_call x1, Pallas kernels: 139 us -> 134 us  [shards(): pl.pallas_call(kernel, out_shape=jax.ShapeDtypeStruct((DOCS // 128, 128),...]
where the time goes in v3:
time: 137 us; the launch traced here: 136 us
  Pallas kernels  134 us (98%)
    pallas_call x1, Pallas kernels, shards(): pl.pallas_call(kernel, out_shape=jax.ShapeDtypeStruct((DOCS // 128, 128),...  134 us

profile of v3, /device:TPU:1, one launch (start us, length us, event | category | flops | bytes accessed | tf_op | source)
XLA Modules:
  0.0 135.5 jit_solution(13510672486964080247)
XLA Ops:
  0.0 134.1 %dedup.1 = f32[50,128]{1,0:T(8,128)} custom-call(s32[6400]{0:T(1024)} %send_hbm.1, s32[6656]{0:T(1024)} %table_hbm.1, bf16[6400,1024]{1,0:T(8,128)(2,1)} %emb_ref.1, s32[50,128]{1,0:T(8,128)} %bitcast.4, s32[50,128]{1,0:T(8,128)} %bitcast.5), custom_call_target="tpu_custom_call" | custom-call | tf_op jit(solution)/shard_map/dedup/pallas_call | solution.py:498
  134.2 1.4 %copy.6 = f32[6400]{0:T(1024)} copy(f32[6400]{0:T(1024)} %bitcast.3) | data formatting | bytes 51200

commit v4 on v3

--- a/solution.py
+++ b/solution.py
@@ -45,15 +45,15 @@
     rep = lax.axis_index("rep")
     z, x, c = me // 8, (me // 2) % 4, me % 2
     def rep_of(r):
-        return (r + 2 * c) % 4
+        return jnp.where(c == 0, r, (4 - r) % 4)
 
     def pick(a, b, c_, d):
         return jnp.where(role == 0, a, jnp.where(role == 1, b, jnp.where(role == 2, c_, d)))
 
     role = rep_of(rep)
     y0 = rep
-    y1 = rep_of(pick(3, 0, 1, 3))
-    y2 = rep_of(pick(0, 2, 3, 0))
+    y1 = rep_of(pick(1, 1, 1, 0))
+    y2 = rep_of(pick(3, 1, 3, 2))
 
     def fetch(ch, slot):
         return pltpu.make_async_copy(
@@ -209,10 +209,13 @@
     def group_of(n):
         return ((x - n // 2 + 4) % 4) * 2 + (z + n) % 2
 
+    def ytarget(n):
+        return rep_of(pick(3, 0, 3, (n % 2) * 2))
+
     def ycopy(n, which):
         g = group_of(n)
         at = jnp.where(role >= 2, 1, 0) if which == 0 else 0
-        dev = rep_of(pick(1, 2, 1, 2)) if which == 0 else rep_of(0)
+        dev = ytarget(n) if which == 0 else rep_of(2)
         return pltpu.make_async_remote_copy(
             src_ref=q.at[0, g, pl.ds(0, GROUP)], dst_ref=q.at[1 + at, g, pl.ds(0, GROUP)],
             send_sem=ysend.at[which, n], recv_sem=yrecv.at[at, n],
@@ -224,7 +227,7 @@
         pltpu.make_async_remote_copy(
             src_ref=q.at[0, g, pl.ds(0, GROUP)], dst_ref=q.at[1 + at, g, pl.ds(0, GROUP)],
             send_sem=ysend.at[0, n], recv_sem=yrecv.at[at, n],
-            device_id={"rep": rep_of(pick(1, 2, 1, 2))}, device_id_type=MESH,
+            device_id={"rep": ytarget(n)}, device_id_type=MESH,
         ).wait_recv()
 
     def arrive(n):
@@ -266,7 +269,7 @@
                     [part[0][j], part[1][j]], axis=0
                 ).astype(BF16)
 
-        @pl.when(role == 3)
+        @pl.when(role == 1)
         def _():
             ycopy(n, 1).start()
 
@@ -294,55 +297,90 @@
             )
         ra[pl.ds(at, GROUP), :] = rows
 
+    half = role // 2
+    splits = (role == 0) | (role == 2)
+
+    def each(count, score):
+        @pl.loop(0, count // 2)
+        def _(m):
+            score(2 * m)
+            score(2 * m + 1)
+
+        @pl.when(count % 2 == 1)
+        def _():
+            score(count - 1)
+
     def before(n):
         g = group_of(n)
 
-        @pl.when(role != 3)
-        def _():
-            @pl.loop(0, n)
-            def _(m):
-                gm = group_of(m)
-                tile(0, g, jnp.where(role == 2, 2, 1), gm, None)
-                tile(0, g, jnp.where(role == 1, 2, 0), gm, None)
-
-        @pl.when(role == 3)
+        @pl.when(role != 1)
+        def _():
+            other = jnp.where(role == 3, 2 - n % 2, 1)
+
+            def score(m):
+                tile(0, g, 0, group_of(m), None)
+                tile(0, g, other, group_of(m), None)
+
+            each(n, score)
+
+        @pl.when(role == 1)
         def _():
             @pl.loop(0, n)
             def _(m):
                 tile(0, g, 0, group_of(m), None)
 
-        @pl.when(role != 1)
-        def _():
-            tile(0, g, 0, g, True)
+        @pl.when(splits)
+        def _():
+            @pl.loop(0, (n + 1 - half) // 2)
+            def _(m):
+                tile(0, g, 2, group_of(2 * m + half), None)
+
+        tile(0, g, 0, g, True)
 
     def after(n):
         g = group_of(n)
 
-        @pl.when(role != 3)
+        @pl.when(splits)
         def _():
             ywait(n, 0)
 
-        @pl.when(role == 0)
-        def _():
-            @pl.loop(0, n + 1)
+            @pl.loop(0, (n + 1 - half) // 2)
             def _(m):
-                tile(0, group_of(m), 1, g, None)
-
-        @pl.when((role == 1) | (role == 2))
-        def _():
+                tile(1, g, 2, group_of(2 * m + half), None)
+
+            @pl.when(n % 2 != half)
+            def _():
+                @pl.loop(0, n + 1)
+                def _(m):
+                    tile(0, group_of(m), 1, g, None)
+
+            @pl.when(n % 2 == half)
+            def _():
+                ywait(n, 1)
+
+                def score(m):
+                    gm = group_of(m)
+                    tile(0, gm, 1, g, None)
+                    tile(0, gm, 2, g, None)
+                    tile(1, gm, 2, g, None)
+
+                each(n + 1, score)
+
+        @pl.when(role == 3)
+        def _():
+            ywait(n, 0)
             ywait(n, 1)
 
-            @pl.loop(0, n)
-            def _(m):
+            def score(m):
                 gm = group_of(m)
-                tile(0, gm, 2, g, None)
                 tile(1, g, 2, gm, None)
                 tile(1, gm, 2, g, None)
-                tile(jnp.where(role == 1, 0, 1), gm, 1, g, None)
-
-            tile(0, g, 2, g, None)
+                tile(0, gm, 2 - m % 2, g, None)
+
+            each(n, score)
+
             tile(1, g, 2, g, None)
-            tile(jnp.where(role == 1, 0, 1), g, 1, g, role == 2)
+            tile(0, g, 2 - n % 2, g, None)
 
     @pl.loop(0, NG + 1)
     def _(n):
@@ -408,7 +446,7 @@
     def _(n):
         ycopy(n, 0).wait_send()
 
-        @pl.when(role == 3)
+        @pl.when(role == 1)
         def _():
             ycopy(n, 1).wait_send()
 

time: 137 us -> 135 us (0.985)
  no operation moved by 1% of the time
where the time goes in v4:
time: 135 us
  Pallas kernels  133 us (99%)
  local copies, waits for them, and re-layouts  1.36 us (1%)
    pallas_call x1, Pallas kernels, shards(): pl.pallas_call(kernel, out_shape=jax.ShapeDtypeStruct((DOCS // 128, 128),...  133 us

profile of v4, /device:TPU:1, one launch (start us, length us, event | category | flops | bytes accessed | tf_op | source)
XLA Modules:
  0.0 134.7 jit_solution(12238116319111991386)
XLA Ops:
  0.0 133.4 %dedup.1 = f32[50,128]{1,0:T(8,128)} custom-call(s32[6400]{0:T(1024)} %send_hbm.1, s32[6656]{0:T(1024)} %table_hbm.1, bf16[6400,1024]{1,0:T(8,128)(2,1)} %emb_ref.1, s32[50,128]{1,0:T(8,128)} %bitcast.4, s32[50,128]{1,0:T(8,128)} %bitcast.5), custom_call_target="tpu_custom_call" | custom-call | tf_op jit(solution)/shard_map/dedup/pallas_call | solution.py:536
  133.4 1.4 %copy.6 = f32[6400]{0:T(1024)} copy(f32[6400]{0:T(1024)} %bitcast.3) | data formatting | bytes 51200
